TPU v7x, 32 devices: a whole 2x2x4 slice. The times are simulated.
32 devices in a mesh: cam: 2 (over x), sp: 16 (over z, y, core).
Axes of the slice: x: 2, y: 2, z: 4, core: 2. Of those that a mesh axis runs over, the one named last changes fastest.
Arguments:
- q_self: bfloat16 [2, 512, 2048], P('cam', 'sp'), may hold values from -8 to 8
- keys: bfloat16 [2, 512, 2048], P('cam', 'sp'), may hold values from -4 to 4
- values: bfloat16 [2, 512, 2048], P('cam', 'sp'), may hold values from -4 to 4
- q_cross: bfloat16 [2, 512, 2048], P('cam', 'sp'), may hold values from -8 to 8
- timestep: int32 [1], replicated, may hold values from 0 to 49
- mod_table: float32 [50, 2, 2048], replicated, may hold values from 0.5 to 3
Outputs:
- block_out: bfloat16 [2, 512, 2048], P('cam', 'sp')
All inputs are finite; a program needn't handle non-finite values.
Results may differ from a plain program's by a relative error of at most 0.0042.
Values may be sent and summed in bfloat16 or wider, within the bound.
A program may use at most 64 MiB of HBM per device.

v0:
```python
import math

import jax
import jax.numpy as jnp
from jax import lax
from jax.sharding import PartitionSpec as P

HEADS = 16


def passed_along(value, axis, steps):
    count = lax.axis_size(axis)
    pairs = [(source, (source + steps) % count) for source in range(count)]
    return lax.ppermute(value, axis, pairs)


def pick_block(extent, ceiling):
    block_size = min(ceiling, extent)
    while extent % block_size:
        block_size = block_size - 1
    return block_size


def attend(queries, key_rows, value_rows, score_scale):
    query_count, head_dim = queries.shape
    key_count = key_rows.shape[0]
    query_block = pick_block(query_count, 512)
    key_block = pick_block(key_count, 1024)
    key_blocks = key_rows.reshape(key_count // key_block, key_block, head_dim)
    value_blocks = value_rows.reshape(key_count // key_block, key_block, head_dim)

    def per_query(query_part):

        def absorb(state_now, pair_now):
            numerator, runmax, totals = state_now
            key_part, value_part = pair_now
            scores = (
                jnp.einsum("qd,kd->qk", query_part, key_part, preferred_element_type=jnp.float32)
                * score_scale
            )
            newmax = jnp.maximum(runmax, jnp.max(scores, axis=1))
            factor = jnp.exp(runmax - newmax)
            weights = jnp.exp(scores - newmax[:, None])
            totals = totals * factor + jnp.sum(weights, axis=1)
            numerator = numerator * factor[:, None] + jnp.dot(
                weights.astype(jnp.bfloat16), value_part, preferred_element_type=jnp.float32
            )
            return ((numerator, newmax, totals), None)

        start_state = (
            jnp.zeros((query_block, head_dim), jnp.float32),
            jnp.full((query_block,), -jnp.inf, jnp.float32),
            jnp.zeros((query_block,), jnp.float32),
        )
        final_state, _ = lax.scan(absorb, start_state, (key_blocks, value_blocks))
        return final_state

    numerator, runmax, totals = lax.map(
        per_query, queries.reshape(query_count // query_block, query_block, head_dim)
    )
    return (
        numerator.reshape(query_count, head_dim),
        runmax.reshape(query_count),
        totals.reshape(query_count),
    )


def local(q_self, keys, values, q_cross, timestep, mod_table):
    row_count = q_self.shape[1]
    full_width = q_self.shape[2]
    head_count = HEADS
    head_dim = full_width // head_count
    groups = lax.axis_size("sp")
    copies = groups // head_count
    part_rows = row_count // copies
    score_scale = 1.0 / math.sqrt(head_dim)
    query_heads = q_self[0].reshape(row_count, head_count, head_dim)
    key_heads = keys[0].reshape(row_count, head_count, head_dim)
    value_heads = values[0].reshape(row_count, head_count, head_dim)

    def quartered(tensor):
        return (
            tensor.reshape(copies, part_rows, head_count, head_dim)
            .transpose(2, 0, 1, 3)
            .reshape(groups, part_rows, head_dim)
        )

    spread = jnp.broadcast_to(
        query_heads.transpose(1, 0, 2)[:, None], (head_count, copies, row_count, head_dim)
    )
    queries_here = lax.all_to_all(
        spread.reshape(groups, row_count, head_dim), "sp", split_axis=0, concat_axis=1, tiled=True
    )
    keys_here = lax.all_to_all(quartered(key_heads), "sp", split_axis=0, concat_axis=1, tiled=True)
    values_here = lax.all_to_all(
        quartered(value_heads), "sp", split_axis=0, concat_axis=1, tiled=True
    )
    numerator, runmax, totals = attend(queries_here[0], keys_here[0], values_here[0], score_scale)
    numerator, runmax, totals = (
        lax.all_to_all(
            numerator.reshape(groups, row_count, head_dim),
            "sp",
            split_axis=0,
            concat_axis=0,
            tiled=True,
        ),
        lax.all_to_all(
            runmax.reshape(groups, row_count), "sp", split_axis=0, concat_axis=0, tiled=True
        ),
        lax.all_to_all(
            totals.reshape(groups, row_count), "sp", split_axis=0, concat_axis=0, tiled=True
        ),
    )
    numerator = numerator.reshape(head_count, copies, row_count, head_dim)
    runmax = runmax.reshape(head_count, copies, row_count)
    totals = totals.reshape(head_count, copies, row_count)
    topmax = jnp.max(runmax, axis=1)
    factor = jnp.exp(runmax - topmax[:, None])
    numerator = jnp.sum(numerator * factor[..., None], axis=1)
    totals = jnp.sum(totals * factor, axis=1)
    self_out = (
        (numerator / totals[..., None])
        .astype(jnp.bfloat16)
        .transpose(1, 0, 2)
        .reshape(row_count, full_width)
    )
    left_keys, left_values = passed_along((keys[0], values[0]), "cam", 1)
    right_keys, right_values = passed_along((keys[0], values[0]), "cam", -1)
    near_keys = jnp.concatenate([left_keys, right_keys], axis=0).reshape(
        2 * row_count, head_count, head_dim
    )
    near_values = jnp.concatenate([left_values, right_values], axis=0).reshape(
        2 * row_count, head_count, head_dim
    )
    cross_queries = q_cross[0].reshape(row_count, head_count, head_dim)
    scores = (
        jnp.einsum("qhd,khd->hqk", cross_queries, near_keys, preferred_element_type=jnp.float32)
        * score_scale
    )
    row_peak = jnp.max(scores, axis=2)
    weights = jnp.exp(scores - row_peak[..., None])
    totals = jnp.sum(weights, axis=2)
    numerator = jnp.einsum(
        "hqk,khd->qhd",
        weights.astype(jnp.bfloat16),
        near_values,
        preferred_element_type=jnp.float32,
    )
    cross_out = (numerator / totals.T[:, :, None]).reshape(row_count, full_width)
    selector = (jnp.arange(mod_table.shape[0]) == timestep[0]).astype(jnp.float32)
    gate_rows = jnp.tensordot(selector, mod_table, axes=1, precision=lax.Precision.HIGHEST)
    mixed = gate_rows[0] * self_out.astype(jnp.float32) + gate_rows[1] * cross_out
    return mixed.astype(jnp.bfloat16)[None]


def solution(mesh):
    placed = (
        P("cam", "sp", None),
        P("cam", "sp", None),
        P("cam", "sp", None),
        P("cam", "sp", None),
        P(),
        P(),
    )
    return jax.shard_map(
        local, mesh=mesh, in_specs=placed, out_specs=P("cam", "sp", None), check_vma=False
    )
```

profile of v0, /device:TPU:0, one launch (start us, length us, event | category | flops | bytes accessed | tf_op | source)
XLA Modules:
  0.0 74.4 jit_solution(12130701770252949441)
XLA Ops:
  0.0 1.0 %copy.35 = bf16[4,8,16,128]{3,2,1,0:T(8,128)(2,1)S(1)} copy(bf16[4,8,16,128]{3,1,2,0:T(8,128)(2,1)} %bitcast.86) | data formatting | bytes 262144
  1.0 0.7 copy.23
  1.7 7.5 %all-to-all-start.1 = ((bf16[16,32,128]{2,1,0:T(8,128)(2,1)}), bf16[16,32,128]{2,1,0:T(8,128)(2,1)S(1)}, u32[]{:S(2)}, u32[]{:S(2)}) async-start(bf16[16,32,128]{2,1,0:T(8,128)(2,1)} %copy.23), calls=%async_computation.1 | async-start | bytes 262144 | tf_op jit(solution)/shard_map/all_to_all | solution.py:94
  9.3 1.6 %collective-permute-start.1 = (bf16[32,2048]{1,0:T(8,128)(2,1)S(1)}, bf16[32,2048]{1,0:T(8,128)(2,1)S(1)}, u32[]{:S(2)}, u32[]{:S(2)}) collective-permute-start(bf16[32,2048]{1,0:T(8,128)(2,1)S(1)} %bitcast.87), channel_id=1, source_target_pairs={{0,16},{16,0},{1,17},{17,1},{2,18},{18,2},{3,19},{19,3},{4,20},{20... | collective-permute-start | bytes 393224 | tf_op jit(solution)/shard_map/ppermute | solution.py:14
  10.8 0.5 collective-permute-start
  11.4 0.7 copy.22
  12.7 0.9 %fusion.4 = f32[1,2,2048]{2,0,1:T(1,128)S(1)} fusion(f32[50,2,2048]{2,1,0:T(2,128)S(1)} %copy-done, s32[]{:T(128)} %bitcast.77), kind=kOutput, calls=%fused_computation.9 | convolution fusion | flops 2457650 | bytes 835588 | tf_op jit(solution)/shard_map/dot_general | solution.py:151
  13.6 3.5 %all-to-all-done.1 = bf16[16,32,128]{2,1,0:T(8,128)(2,1)S(1)} async-done(((bf16[16,32,128]{2,1,0:T(8,128)(2,1)}), bf16[16,32,128]{2,1,0:T(8,128)(2,1)S(1)}, u32[]{:S(2)}, u32[]{:S(2)}) %all-to-all-start.1) | async-done | bytes 131104 | tf_op jit(solution)/shard_map/all_to_all | solution.py:94
  17.2 3.5 %all-to-all-start = ((bf16[16,32,128]{2,1,0:T(8,128)(2,1)}), bf16[16,32,128]{2,1,0:T(8,128)(2,1)S(1)}, u32[]{:S(2)}, u32[]{:S(2)}) async-start(bf16[16,32,128]{2,1,0:T(8,128)(2,1)} %copy.22), calls=%async_computation | async-start | bytes 262144 | tf_op jit(solution)/shard_map/all_to_all | solution.py:91
  20.7 0.7 copy.24
  21.4 0.2 copy-done.2
  21.7 0.3 fusion.23
  22.0 6.6 %all-to-all-done = bf16[16,32,128]{2,1,0:T(8,128)(2,1)S(1)} async-done(((bf16[16,32,128]{2,1,0:T(8,128)(2,1)}), bf16[16,32,128]{2,1,0:T(8,128)(2,1)S(1)}, u32[]{:S(2)}, u32[]{:S(2)}) %all-to-all-start) | async-done | bytes 131104 | tf_op jit(solution)/shard_map/all_to_all | solution.py:91
  28.6 3.5 %all-to-all-start.2 = ((bf16[16,32,128]{2,1,0:T(8,128)(2,1)}), bf16[16,32,128]{2,1,0:T(8,128)(2,1)S(1)}, u32[]{:S(2)}, u32[]{:S(2)}) async-start(bf16[16,32,128]{2,1,0:T(8,128)(2,1)} %copy.24), calls=%async_computation.2 | async-start | bytes 262144 | tf_op jit(solution)/shard_map/all_to_all | solution.py:95
  32.1 0.3 fusion.24
  32.4 0.2 fusion.2
  32.6 0.7 all_to_all.38
  33.4 1.3 %multiply_add_fusion = f32[16,1,32]{2,1,0:T(1,128)} fusion(f32[16,1,32]{2,1,0:T(1,128)S(1)} %reduce_sum.28, f32[16,1,32]{2,1,0:T(1,128)} %all_to_all.38), kind=kLoop, calls=%fused_computation.29 | loop fusion | flops 1536 | bytes 6144 | tf_op jit(solution)/shard_map/while/body/eval_jaxpr/while/body/eval_jaxpr/add | solution.py:44
  34.7 5.3 %all-to-all-done.2 = bf16[16,32,128]{2,1,0:T(8,128)(2,1)S(1)} async-done(((bf16[16,32,128]{2,1,0:T(8,128)(2,1)}), bf16[16,32,128]{2,1,0:T(8,128)(2,1)S(1)}, u32[]{:S(2)}, u32[]{:S(2)}) %all-to-all-start.2) | async-done | bytes 131104 | tf_op jit(solution)/shard_map/all_to_all | solution.py:95
  40.0 3.5 %all-to-all-start.5 = ((f32[16,1,32]{2,1,0:T(1,128)}), f32[16,1,32]{2,1,0:T(1,128)S(1)}, u32[]{:S(2)}, u32[]{:S(2)}) async-start(f32[16,1,32]{2,1,0:T(1,128)} %multiply_add_fusion), calls=%async_computation.5 | async-start | bytes 16384 | tf_op jit(solution)/shard_map/all_to_all | solution.py:110
  43.5 6.4 %all-to-all-done.5 = f32[16,1,32]{2,1,0:T(1,128)S(1)} async-done(((f32[16,1,32]{2,1,0:T(1,128)}), f32[16,1,32]{2,1,0:T(1,128)S(1)}, u32[]{:S(2)}, u32[]{:S(2)}) %all-to-all-start.5) | async-done | bytes 2080 | tf_op jit(solution)/shard_map/all_to_all | solution.py:110
  49.9 3.5 %all-to-all-start.4 = ((f32[16,1,32]{2,1,0:T(1,128)}), f32[16,1,32]{2,1,0:T(1,128)S(1)}, u32[]{:S(2)}, u32[]{:S(2)}) async-start(f32[16,1,32]{2,1,0:T(1,128)} %all_to_all.38), calls=%async_computation.4 | async-start | bytes 16384 | tf_op jit(solution)/shard_map/all_to_all | solution.py:107
  53.4 1.0 %convolution_add_fusion = f32[512,128]{1,0:T(8,128)} fusion(bf16[512,128]{1,0:T(8,128)(2,1)S(1)} %bitcast.83, f32[512,512]{0,1:T(8,128)S(1)} %get-tuple-element.61, f32[512]{0:T(512)S(1)} %get-tuple-element.60, f32[512]{0:T(512)S(1)} %exponential_multiply_fusion), kind=kOutput, calls=%fused_computation.5 | convolution fusion | flops 67698688 | bytes 1445888 | tf_op jit(solution)/shard_map/while/body/eval_jaxpr/while/body/eval_jaxpr/dot_general | solution.py:45
  54.4 5.3 %all-to-all-done.4 = f32[16,1,32]{2,1,0:T(1,128)S(1)} async-done(((f32[16,1,32]{2,1,0:T(1,128)}), f32[16,1,32]{2,1,0:T(1,128)S(1)}, u32[]{:S(2)}, u32[]{:S(2)}) %all-to-all-start.4) | async-done | bytes 2080 | tf_op jit(solution)/shard_map/all_to_all | solution.py:107
  59.7 3.5 %all-to-all-start.3 = ((f32[16,32,128]{2,1,0:T(8,128)}), f32[16,32,128]{2,1,0:T(8,128)S(1)}, u32[]{:S(2)}, u32[]{:S(2)}) async-start(f32[16,32,128]{2,1,0:T(8,128)} %bitcast.12), calls=%async_computation.3 | async-start | bytes 524288 | tf_op jit(solution)/shard_map/all_to_all | solution.py:100
  63.3 0.3 fusion.12
  63.5 0.3 fusion
  63.8 0.2 copy.29
  64.1 9.2 %all-to-all-done.3 = f32[16,32,128]{2,1,0:T(8,128)S(1)} async-done(((f32[16,32,128]{2,1,0:T(8,128)}), f32[16,32,128]{2,1,0:T(8,128)S(1)}, u32[]{:S(2)}, u32[]{:S(2)}) %all-to-all-start.3) | async-done | bytes 262176 | tf_op jit(solution)/shard_map/all_to_all | solution.py:100
  73.3 0.2 convert_bitcast_fusion
  73.5 0.2 copy.25
  73.7 0.7 add_convert_fusion
  (23 shorter events, 0.3 us)
Async XLA Ops:
  0.0 12.7 %copy-start = (f32[50,2,2048]{2,1,0:T(2,128)S(1)}, f32[50,2,2048]{2,1,0:T(2,128)}, u32[]{:S(2)}) copy-start(f32[50,2,2048]{2,1,0:T(2,128)} %param.11) | copy-start | bytes 2457604
  1.0 9.8 %copy-start.4 = (bf16[1,32,2048]{2,1,0:T(8,128)(2,1)S(1)}, bf16[1,32,2048]{2,1,0:T(8,128)(2,1)}, u32[]{:S(2)}) copy-start(bf16[1,32,2048]{2,1,0:T(8,128)(2,1)} %param.8) | copy-start | bytes 393220
  1.7 7.5 %copy-start.3 = (bf16[1,32,2048]{2,1,0:T(8,128)(2,1)S(1)}, bf16[1,32,2048]{2,1,0:T(8,128)(2,1)}, u32[]{:S(2)}) copy-start(bf16[1,32,2048]{2,1,0:T(8,128)(2,1)} %param.7) | copy-start | bytes 393220
  1.7 9.6 %copy-start.1 = (bf16[1,32,2048]{2,1,0:T(8,128)(2,1)S(1)}, bf16[1,32,2048]{2,1,0:T(8,128)(2,1)}, u32[]{:S(2)}) copy-start(bf16[1,32,2048]{2,1,0:T(8,128)(2,1)} %param.6) | copy-start | bytes 393220
  1.7 15.5 %all-to-all-start.1 = ((bf16[16,32,128]{2,1,0:T(8,128)(2,1)}), bf16[16,32,128]{2,1,0:T(8,128)(2,1)S(1)}, u32[]{:S(2)}, u32[]{:S(2)}) async-start(bf16[16,32,128]{2,1,0:T(8,128)(2,1)} %copy.23), calls=%async_computation.1 | async-start | bytes 262144 | tf_op jit(solution)/shard_map/all_to_all | solution.py:94
  9.3 12.4 %collective-permute-start.1 = (bf16[32,2048]{1,0:T(8,128)(2,1)S(1)}, bf16[32,2048]{1,0:T(8,128)(2,1)S(1)}, u32[]{:S(2)}, u32[]{:S(2)}) collective-permute-start(bf16[32,2048]{1,0:T(8,128)(2,1)S(1)} %bitcast.87), channel_id=1, source_target_pairs={{0,16},{16,0},{1,17},{17,1},{2,18},{18,2},{3,19},{19,3},{4,20},{20... | collective-permute-start | bytes 393224 | tf_op jit(solution)/shard_map/ppermute | solution.py:14
  10.8 52.7 %collective-permute-start = (bf16[32,2048]{1,0:T(8,128)(2,1)S(1)}, bf16[32,2048]{1,0:T(8,128)(2,1)S(1)}, u32[]{:S(2)}, u32[]{:S(2)}) collective-permute-start(bf16[32,2048]{1,0:T(8,128)(2,1)S(1)} %bitcast.88), channel_id=1, source_target_pairs={{0,16},{16,0},{1,17},{17,1},{2,18},{18,2},{3,19},{19,3},{4,20},{20... | collective-permute-start | bytes 393224 | tf_op jit(solution)/shard_map/ppermute | solution.py:14
  17.2 11.4 %all-to-all-start = ((bf16[16,32,128]{2,1,0:T(8,128)(2,1)}), bf16[16,32,128]{2,1,0:T(8,128)(2,1)S(1)}, u32[]{:S(2)}, u32[]{:S(2)}) async-start(bf16[16,32,128]{2,1,0:T(8,128)(2,1)} %copy.22), calls=%async_computation | async-start | bytes 262144 | tf_op jit(solution)/shard_map/all_to_all | solution.py:91
  20.7 0.9 %copy-start.2 = (bf16[1,32,2048]{2,1,0:T(8,128)(2,1)S(1)}, bf16[1,32,2048]{2,1,0:T(8,128)(2,1)}, u32[]{:S(2)}) copy-start(bf16[1,32,2048]{2,1,0:T(8,128)(2,1)} %param.9) | copy-start | bytes 393220
  28.6 11.4 %all-to-all-start.2 = ((bf16[16,32,128]{2,1,0:T(8,128)(2,1)}), bf16[16,32,128]{2,1,0:T(8,128)(2,1)S(1)}, u32[]{:S(2)}, u32[]{:S(2)}) async-start(bf16[16,32,128]{2,1,0:T(8,128)(2,1)} %copy.24), calls=%async_computation.2 | async-start | bytes 262144 | tf_op jit(solution)/shard_map/all_to_all | solution.py:95
  40.0 9.9 %all-to-all-start.5 = ((f32[16,1,32]{2,1,0:T(1,128)}), f32[16,1,32]{2,1,0:T(1,128)S(1)}, u32[]{:S(2)}, u32[]{:S(2)}) async-start(f32[16,1,32]{2,1,0:T(1,128)} %multiply_add_fusion), calls=%async_computation.5 | async-start | bytes 16384 | tf_op jit(solution)/shard_map/all_to_all | solution.py:110
  49.9 9.8 %all-to-all-start.4 = ((f32[16,1,32]{2,1,0:T(1,128)}), f32[16,1,32]{2,1,0:T(1,128)S(1)}, u32[]{:S(2)}, u32[]{:S(2)}) async-start(f32[16,1,32]{2,1,0:T(1,128)} %all_to_all.38), calls=%async_computation.4 | async-start | bytes 16384 | tf_op jit(solution)/shard_map/all_to_all | solution.py:107
  59.7 13.5 %all-to-all-start.3 = ((f32[16,32,128]{2,1,0:T(8,128)}), f32[16,32,128]{2,1,0:T(8,128)S(1)}, u32[]{:S(2)}, u32[]{:S(2)}) async-start(f32[16,32,128]{2,1,0:T(8,128)} %bitcast.12), calls=%async_computation.3 | async-start | bytes 524288 | tf_op jit(solution)/shard_map/all_to_all | solution.py:100
where the time goes:
time: 75.1 us; the launch traced here: 74.4 us
  waiting for transfers between devices  36.4 us (48%)
  starting transfers between devices  27.1 us (36%)
  local copies, waits for them, and re-layouts  4.56 us (6%)
  matrix products  2.81 us (4%)
  other arithmetic  2.68 us (4%)
  between operations  0.87 us (1%)
    all_to_all x1, waiting for transfers between devices, local(): lax.all_to_all(numerator.reshape(groups, row_count, head_dim), 'sp', spli...  9.22 us
    all_to_all x1, starting transfers between devices, local(): lax.all_to_all(quartered(key_heads), 'sp', split_axis=0, concat_axis=1, t...  7.52 us
    all_to_all x1, waiting for transfers between devices, local(): lax.all_to_all(spread.reshape(groups, row_count, head_dim), 'sp', split_a...  6.6 us
    all_to_all x1, waiting for transfers between devices, local(): lax.all_to_all(totals.reshape(groups, row_count), 'sp', split_axis=0, con...  6.36 us
    all_to_all x1, waiting for transfers between devices, local(): lax.all_to_all(quartered(value_heads), 'sp', split_axis=0, concat_axis=1,...  5.32 us
    all_to_all x1, waiting for transfers between devices, local(): lax.all_to_all(runmax.reshape(groups, row_count), 'sp', split_axis=0, con...  5.31 us
    all_to_all x1, waiting for transfers between devices, local(): lax.all_to_all(quartered(key_heads), 'sp', split_axis=0, concat_axis=1, t...  3.55 us
    all_to_all x1, starting transfers between devices, local(): lax.all_to_all(numerator.reshape(groups, row_count, head_dim), 'sp', spli...  3.53 us
  transfers between devices with their start and end apart: 8, of which 6 were waited for; matrix products, arithmetic and copies ran while one was open for 9% of the time, Pallas kernels for 0%

commit v1 on v0

v1 whole, which is shorter than its diff:
```python
import functools
import math

import jax
import jax.numpy as jnp
from jax import lax
from jax.experimental import pallas as pl
from jax.experimental.pallas import tpu as pltpu
from jax.sharding import PartitionSpec as P

HEADS = 16
MESH = pl.DeviceIdType.MESH
LOG2E = 1.4426950408889634


def offsets(count):
    return sorted(range(1, count), key=lambda d: (abs(d - count // 2), d))


def softmax_parts(scores, scale):
    peak = jnp.max(scores, axis=-1, keepdims=True)
    weights = jnp.exp2((scores - peak) * (scale * LOG2E))
    return weights.astype(jnp.bfloat16), jnp.sum(weights, axis=-1, keepdims=True)


def dot_t(a, b):
    return lax.dot_general(a, b, (((1,), (1,)), ((), ())), preferred_element_type=jnp.float32)


def kernel(
    n, cams, step_ref, q_ref, k_ref, v_ref, qc_ref, mod_ref, out_ref,
    q_all, k_all, v_all, near_k, near_v, qc, mod, weights, sums, mine, back, cross,
    send_sem, cross_send, back_send, q_sem, k_sem, v_sem, near_sem, back_sem, qc_sem, mod_sem,
):
    rows, dim = q_all.shape[1], q_all.shape[2]
    heads = HEADS
    copies = n // heads
    sides = near_k.shape[0]
    me = lax.axis_index("sp")
    cam = lax.axis_index("cam")
    head = lax.div(me, copies)
    copy = lax.rem(me, copies)
    my_group = lax.div(me, heads)
    my_slot = lax.rem(me, heads)
    scale = 1.0 / math.sqrt(dim)

    def cols(h):
        return pl.ds(pl.multiple_of(h * dim, dim), dim)

    barrier = pltpu.get_barrier_semaphore()
    for d in offsets(n):
        pl.semaphore_signal(
            barrier, inc=1, device_id={"sp": lax.rem(me + d, n)}, device_id_type=MESH
        )
    for side in range(sides):
        other = lax.rem(cam + (1 if side == 0 else cams - 1), cams)
        pl.semaphore_signal(barrier, inc=1, device_id={"cam": other}, device_id_type=MESH)

    load_qc = pltpu.make_async_copy(qc_ref.at[0], qc, qc_sem)
    load_mod = pltpu.make_async_copy(mod_ref, mod, mod_sem)
    load_qc.start()
    load_mod.start()
    pltpu.make_async_copy(k_ref.at[0, :, cols(head)], k_all.at[me], k_sem).start()
    pltpu.make_async_copy(v_ref.at[0, :, cols(head)], v_all.at[me], v_sem).start()
    in_group = my_group == copy

    @pl.when(in_group)
    def _():
        pltpu.make_async_copy(q_ref.at[0, :, cols(head)], q_all.at[my_slot], q_sem).start()

    pl.semaphore_wait(barrier, n - 1 + sides)

    def send(src, dst, sem, peer):
        pltpu.make_async_remote_copy(
            src_ref=src, dst_ref=dst, send_sem=send_sem, recv_sem=sem,
            device_id={"sp": peer}, device_id_type=MESH,
        ).start()

    for d in offsets(n):
        peer = lax.rem(me + d, n)
        send(k_ref.at[0, :, cols(lax.div(peer, copies))], k_all.at[me], k_sem, peer)
        if copies == 1:
            send(q_ref.at[0, :, cols(peer)], q_all.at[me], q_sem, peer)
    if copies > 1:
        for h in range(heads):
            peer = h * copies + my_group

            @pl.when(peer != me)
            def _():
                send(q_ref.at[0, :, cols(h)], q_all.at[my_slot], q_sem, peer)

    for side in range(sides):
        other = lax.rem(cam + (1 if side == 0 else cams - 1), cams)
        for index, (src, dst) in enumerate(((k_ref, near_k), (v_ref, near_v))):
            pltpu.make_async_remote_copy(
                src_ref=src.at[0], dst_ref=dst.at[side],
                send_sem=cross_send.at[side, index], recv_sem=near_sem.at[side, index],
                device_id={"cam": other}, device_id_type=MESH,
            ).start()
    for d in offsets(n):
        peer = lax.rem(me + d, n)
        send(v_ref.at[0, :, cols(lax.div(peer, copies))], v_all.at[me], v_sem, peer)

    load_qc.wait()
    load_mod.wait()
    for side in range(sides):
        for index, dst in enumerate((near_k, near_v)):
            pltpu.make_async_copy(dst.at[side], dst.at[side], near_sem.at[side, index]).wait()
    gates = mod[step_ref[0]]
    for h in range(heads):
        part = slice(h * dim, (h + 1) * dim)
        keys = near_k[:, :, part].reshape(sides * rows, dim)
        vals = near_v[:, :, part].reshape(sides * rows, dim)
        w, total = softmax_parts(dot_t(qc[:, part], keys), scale)
        result = jnp.dot(w, vals, preferred_element_type=jnp.float32) / total
        cross[:, part] = gates[1:2, part] * result

    pltpu.make_async_copy(k_all, k_all, k_sem).wait()
    pltpu.make_async_copy(q_all, q_all, q_sem).wait()
    per = 4
    blocks = heads // per
    first = lax.div(my_slot, per)
    order = [blocks // 2] + [b for b in range(1, blocks) if b != blocks // 2] + [0]
    keys = k_all[...].reshape(n * rows, dim)
    for index, b in enumerate(order):
        block = lax.rem(first + b, blocks)
        queries = q_all[pl.ds(block * per, per)].reshape(per * rows, dim)
        w, total = softmax_parts(dot_t(queries, keys), scale)
        weights[index] = w
        sums[index] = total
    pltpu.make_async_copy(v_all, v_all, v_sem).wait()
    vals = v_all[...].reshape(n * rows, dim)
    for index, b in enumerate(order):
        block = lax.rem(first + b, blocks)
        result = jnp.dot(weights[index], vals, preferred_element_type=jnp.float32) / sums[index]
        mine[pl.ds(block * per, per)] = result.astype(jnp.bfloat16).reshape(per, rows, dim)
        for s in range(per):
            slot = block * per + s
            peer = copy * heads + slot

            @pl.when(peer != me)
            def _():
                pltpu.make_async_remote_copy(
                    src_ref=mine.at[slot], dst_ref=back.at[head],
                    send_sem=back_send, recv_sem=back_sem,
                    device_id={"sp": peer}, device_id_type=MESH,
                ).start()

            @pl.when(peer == me)
            def _():
                pltpu.make_async_copy(mine.at[slot], back.at[head], back_sem).start()

    pltpu.make_async_copy(back, back, back_sem).wait()
    for h in range(heads):
        part = slice(h * dim, (h + 1) * dim)
        mixed = gates[0:1, part] * back[h].astype(jnp.float32) + cross[:, part]
        out_ref[0, :, part] = mixed.astype(out_ref.dtype)

    for dst in (k_all, v_all):
        sent = dst.at[pl.ds(0, n - 1)]
        pltpu.make_async_copy(sent, sent, send_sem).wait()
    for side in range(sides):
        for index, dst in enumerate((near_k, near_v)):
            pltpu.make_async_copy(dst.at[side], dst.at[side], cross_send.at[side, index]).wait()
    for buffer, sem in ((q_all, send_sem), (mine, back_send)):

        @pl.when(in_group)
        def _():
            sent = buffer.at[pl.ds(0, heads - 1)]
            pltpu.make_async_copy(sent, sent, sem).wait()

        if copies > 1:

            @pl.when(jnp.logical_not(in_group))
            def _():
                pltpu.make_async_copy(buffer, buffer, sem).wait()


def solution(mesh):
    n, cams = mesh.shape["sp"], mesh.shape["cam"]
    sides = 1 if cams == 2 else 2

    def local(q_self, keys, values, q_cross, timestep, mod_table):
        rows, width = q_self.shape[1], q_self.shape[2]
        dim = width // HEADS
        bf16, f32 = jnp.bfloat16, jnp.float32
        per = 4
        blocks = HEADS // per
        hbm = pl.BlockSpec(memory_space=pl.ANY)
        return pl.pallas_call(
            functools.partial(kernel, n, cams),
            out_shape=jax.ShapeDtypeStruct(q_self.shape, bf16),
            in_specs=[pl.BlockSpec(memory_space=pltpu.SMEM)] + [hbm] * 5,
            out_specs=pl.BlockSpec(memory_space=pltpu.VMEM),
            scratch_shapes=[
                pltpu.VMEM((HEADS, rows, dim), bf16),
                pltpu.VMEM((n, rows, dim), bf16),
                pltpu.VMEM((n, rows, dim), bf16),
                pltpu.VMEM((sides, rows, width), bf16),
                pltpu.VMEM((sides, rows, width), bf16),
                pltpu.VMEM((rows, width), bf16),
                pltpu.VMEM(mod_table.shape, f32),
                pltpu.VMEM((blocks, per * rows, n * rows), bf16),
                pltpu.VMEM((blocks, per * rows, 1), f32),
                pltpu.VMEM((HEADS, rows, dim), bf16),
                pltpu.VMEM((HEADS, rows, dim), bf16),
                pltpu.VMEM((rows, width), f32),
                pltpu.SemaphoreType.DMA,
                pltpu.SemaphoreType.DMA((sides, 2)),
                pltpu.SemaphoreType.DMA,
                pltpu.SemaphoreType.DMA,
                pltpu.SemaphoreType.DMA,
                pltpu.SemaphoreType.DMA,
                pltpu.SemaphoreType.DMA((sides, 2)),
                pltpu.SemaphoreType.DMA,
                pltpu.SemaphoreType.DMA,
                pltpu.SemaphoreType.DMA,
            ],
            compiler_params=pltpu.CompilerParams(
                collective_id=0, has_side_effects=True, vmem_limit_bytes=60 * 1024 * 1024
            ),
        )(timestep, q_self, keys, values, q_cross, mod_table)

    placed = P("cam", "sp", None)
    return jax.shard_map(
        local,
        mesh=mesh,
        in_specs=(placed, placed, placed, placed, P(), P()),
        out_specs=placed,
        check_vma=False,
    )
```

time: 75.1 us -> 24.9 us (0.33)
  waiting for transfers between devices: 36.4 us -> 0 us
  starting transfers between devices: 27.1 us -> 0 us
  Pallas kernels: 0 us -> 22.6 us
  local copies, waits for them, and re-layouts: 4.56 us -> 1.57 us
  matrix products: 2.81 us -> 0 us
  other arithmetic: 2.68 us -> 0 us
    all_to_all x6 -> x0, waiting for transfers between devices: 36.4 us -> none  [the longest x1 9.22 us: local(): lax.all_to_all(numerator.reshape(groups, row_count, head_dim), 'sp', spli...]
    all_to_all x6 -> x0, starting transfers between devices: 25 us -> none  [the longest x1 7.52 us: local(): lax.all_to_all(quartered(key_heads), 'sp', split_axis=0, concat_axis=1, t...]
    pallas_call x0 -> x1, Pallas kernels: none -> 22.6 us  [local(): pl.pallas_call(functools.partial(kernel, n, cams), out_shape=jax.ShapeDty...]
    dot_general x5 -> x0, matrix products: 2.81 us -> none  [the longest x1 1.05 us: absorb(): jnp.dot(weights.astype(jnp.bfloat16), value_part, preferred_element_type=...]
    ppermute x2 -> x0, starting transfers between devices: 2.09 us -> none  [passed_along(): return lax.ppermute(value, axis, pairs)]
    reshape x5 -> x0, local copies, waits for them, and re-layouts: 1.45 us -> none  [the longest x4 1.4 us: quartered(): return tensor.reshape(copies, part_rows, head_count, head_dim).transpose(...]
    add x1 -> x0, other arithmetic: 1.31 us -> none  [absorb(): totals = totals * factor + jnp.sum(weights, axis=1)]
    convert_element_type x2 -> x0, other arithmetic: 0.9 us -> none  [the longest x1 0.7 us: local(): return mixed.astype(jnp.bfloat16)[None]]
  transfers between devices with their start and end apart: 8 -> 0, of which waited for: 6 -> 0; matrix products, arithmetic and copies ran while one was open for 9% -> 0% of each run, Pallas kernels for 0% -> 0%
where the time goes in v1:
time: 24.9 us; the launch traced here: 24.8 us
  Pallas kernels  22.6 us (91%)
  local copies, waits for them, and re-layouts  1.57 us (6%)
  between operations  0.66 us (3%)
    pallas_call x1, Pallas kernels, local(): pl.pallas_call(functools.partial(kernel, n, cams), out_shape=jax.ShapeDty...  22.6 us
    unnamed x1, local copies, waits for them, and re-layouts  1.57 us

profile of v1, /device:TPU:0, one launch (start us, length us, event | category | flops | bytes accessed | tf_op | source)
XLA Modules:
  0.0 24.8 jit_solution(7924336181551427423)
XLA Ops:
  0.7 22.6 %shard_map.64 = bf16[1,32,2048]{2,1,0:T(8,128)(2,1)} custom-call(s32[1]{0:T(128)S(6)} %copy.8.step_ref, bf16[1,32,2048]{2,1,0:T(8,128)(2,1)} %q_ref.1, bf16[1,32,2048]{2,1,0:T(8,128)(2,1)} %k_ref.1, bf16[1,32,2048]{2,1,0:T(8,128)(2,1)} %v_ref.1, bf16[1,32,2048]{2,1,0:T(8,128)(2,1)} %qc_ref.1, f32[50,2,2048]{2,1,0:T(2,128)} %mod_ref.1), custom_call_target="tpu_custom_call" | custom-call | tf_op jit(solution)/shard_map/pallas_call | solution.py:190
  23.2 1.6 %copy.9 = bf16[1,32,2048]{2,1,0:T(8,128)(2,1)} copy(bf16[1,32,2048]{2,1,0:T(8,128)(2,1)} %shard_map.64) | data formatting | bytes 262144

commit v2 on v1

v2 whole, which is shorter than its diff:
```python
import functools
import math

import jax
import jax.numpy as jnp
from jax import lax
from jax.experimental import pallas as pl
from jax.experimental.pallas import tpu as pltpu
from jax.sharding import PartitionSpec as P

HEADS = 16
GROUPS = 4
MESH = pl.DeviceIdType.MESH
LOG2E = 1.4426950408889634


def offsets(count):
    return sorted(range(1, count), key=lambda d: (-abs(d - count // 2), d))


def softmax_parts(scores, scale):
    peak = jnp.max(scores, axis=-1, keepdims=True)
    weights = jnp.exp2((scores - peak) * (scale * LOG2E))
    return weights.astype(jnp.bfloat16), jnp.sum(weights, axis=-1, keepdims=True)


def dot_t(a, b):
    return lax.dot_general(a, b, (((1,), (1,)), ((), ())), preferred_element_type=jnp.float32)


def kernel(
    n, cams, step_in, q_ref, k_ref, v_ref, qc_ref, mod_ref, out_ref,
    q_all, k_all, v_all, near_k, near_v, qc, mod, step_ref, mine, back, cross,
    send_sem, cross_send, back_send, q_sem, k_sem, v_sem, near_sem, back_sem, qc_sem, mod_sem, step_sem,
):
    rows, dim = q_all.shape[1], q_all.shape[2]
    heads = HEADS
    copies = n // heads
    sides = near_k.shape[0]
    me = lax.axis_index("sp")
    cam = lax.axis_index("cam")
    head = lax.div(me, copies)
    copy = lax.rem(me, copies)
    my_group = lax.div(me, heads)
    my_slot = lax.rem(me, heads)
    scale = 1.0 / math.sqrt(dim)
    order = offsets(heads) + [0]
    groups = q_sem.shape[0]
    per = heads // groups

    def cols(h):
        return pl.ds(pl.multiple_of(h * dim, dim), dim)

    barrier = pltpu.get_barrier_semaphore()
    for d in offsets(n):
        pl.semaphore_signal(
            barrier, inc=1, device_id={"sp": lax.rem(me + d, n)}, device_id_type=MESH
        )
    for side in range(sides):
        other = lax.rem(cam + (1 if side == 0 else cams - 1), cams)
        pl.semaphore_signal(barrier, inc=1, device_id={"cam": other}, device_id_type=MESH)

    load_qc = pltpu.make_async_copy(qc_ref.at[0], qc, qc_sem)
    load_mod = pltpu.make_async_copy(mod_ref, mod, mod_sem)
    load_qc.start()
    load_mod.start()
    load_step = pltpu.make_async_copy(step_in, step_ref, step_sem)
    load_step.start()
    pltpu.make_async_copy(k_ref.at[0, :, cols(head)], k_all.at[me], k_sem).start()
    pltpu.make_async_copy(v_ref.at[0, :, cols(head)], v_all.at[me], v_sem).start()
    pl.semaphore_wait(barrier, n - 1 + sides)

    def send(src, dst, sem, peer):
        pltpu.make_async_remote_copy(
            src_ref=src, dst_ref=dst, send_sem=send_sem, recv_sem=sem,
            device_id={"sp": peer}, device_id_type=MESH,
        ).start()

    for src, dst, sem in ((k_ref, k_all, k_sem), (v_ref, v_all, v_sem)):
        for d in offsets(n):
            peer = lax.rem(me + d, n)
            send(src.at[0, :, cols(lax.div(peer, copies))], dst.at[me], sem, peer)

    def by_place(d, peer, far, near):
        if copies == 1:
            (far if d else near)()
        else:
            pl.when(peer != me)(far)
            pl.when(peer == me)(near)

    for i, d in enumerate(order):
        target = lax.rem(my_slot + d, heads)
        peer = target * copies + my_group
        src, dst, sem = q_ref.at[0, :, cols(target)], q_all.at[i], q_sem.at[i // per]
        by_place(
            d, peer,
            lambda: send(src, dst, sem, peer),
            lambda: pltpu.make_async_copy(src, dst, sem).start(),
        )

    for side in range(sides):
        other = lax.rem(cam + (1 if side == 0 else cams - 1), cams)
        for index, (src, dst) in enumerate(((k_ref, near_k), (v_ref, near_v))):
            pltpu.make_async_remote_copy(
                src_ref=src.at[0], dst_ref=dst.at[side],
                send_sem=cross_send.at[side, index], recv_sem=near_sem.at[side, index],
                device_id={"cam": other}, device_id_type=MESH,
            ).start()
    pltpu.make_async_copy(k_all, k_all, k_sem).wait()
    pltpu.make_async_copy(v_all, v_all, v_sem).wait()
    keys = k_all[...].reshape(n * rows, dim)
    vals = v_all[...].reshape(n * rows, dim)
    for g in range(groups):
        here = pl.ds(g * per, per)
        pltpu.make_async_copy(q_all.at[here], q_all.at[here], q_sem.at[g]).wait()
        w, total = softmax_parts(dot_t(q_all[here].reshape(per * rows, dim), keys), scale)
        result = jnp.dot(w, vals, preferred_element_type=jnp.float32) / total
        mine[here] = result.astype(jnp.bfloat16).reshape(per, rows, dim)
        for i in range(g * per, (g + 1) * per):
            d = order[i]
            peer = copy * heads + lax.rem(head + heads - d, heads)
            src, dst = mine.at[i], back.at[head]
            by_place(
                d, peer,
                lambda: pltpu.make_async_remote_copy(
                    src_ref=src, dst_ref=dst, send_sem=back_send, recv_sem=back_sem,
                    device_id={"sp": peer}, device_id_type=MESH,
                ).start(),
                lambda: pltpu.make_async_copy(src, dst, back_sem).start(),
            )

    load_qc.wait()
    load_mod.wait()
    load_step.wait()
    for side in range(sides):
        for index, dst in enumerate((near_k, near_v)):
            pltpu.make_async_copy(dst.at[side], dst.at[side], near_sem.at[side, index]).wait()
    gates = mod[step_ref[0]]
    for h in range(heads):
        part = slice(h * dim, (h + 1) * dim)
        keys = near_k[:, :, part].reshape(sides * rows, dim)
        vals = near_v[:, :, part].reshape(sides * rows, dim)
        w, total = softmax_parts(dot_t(qc[:, part], keys), scale)
        result = jnp.dot(w, vals, preferred_element_type=jnp.float32) / total
        cross[:, part] = gates[1:2, part] * result

    pltpu.make_async_copy(back, back, back_sem).wait()
    for h in range(heads):
        part = slice(h * dim, (h + 1) * dim)
        mixed = gates[0:1, part] * back[h].astype(jnp.float32) + cross[:, part]
        out_ref[0, :, part] = mixed.astype(out_ref.dtype)

    for dst in (k_all, v_all):
        sent = dst.at[pl.ds(0, n - 1)]
        pltpu.make_async_copy(sent, sent, send_sem).wait()
    for side in range(sides):
        for index, dst in enumerate((near_k, near_v)):
            pltpu.make_async_copy(dst.at[side], dst.at[side], cross_send.at[side, index]).wait()
    for buffer, sem in ((q_all, send_sem), (mine, back_send)):
        sent = buffer.at[pl.ds(0, heads - 1)]
        rest = buffer.at[0]
        pltpu.make_async_copy(sent, sent, sem).wait()
        if copies > 1:

            @pl.when(my_group != copy)
            def _():
                pltpu.make_async_copy(rest, rest, sem).wait()


def solution(mesh):
    n, cams = mesh.shape["sp"], mesh.shape["cam"]
    sides = 1 if cams == 2 else 2

    def local(q_self, keys, values, q_cross, timestep, mod_table):
        rows, width = q_self.shape[1], q_self.shape[2]
        dim = width // HEADS
        bf16, f32 = jnp.bfloat16, jnp.float32
        hbm = pl.BlockSpec(memory_space=pl.ANY)
        return pl.pallas_call(
            functools.partial(kernel, n, cams),
            out_shape=pltpu.VMEM(q_self.shape, bf16),
            in_specs=[hbm] * 6,
            out_specs=pl.BlockSpec(memory_space=pltpu.VMEM),
            scratch_shapes=[
                pltpu.VMEM((HEADS, rows, dim), bf16),
                pltpu.VMEM((n, rows, dim), bf16),
                pltpu.VMEM((n, rows, dim), bf16),
                pltpu.VMEM((sides, rows, width), bf16),
                pltpu.VMEM((sides, rows, width), bf16),
                pltpu.VMEM((rows, width), bf16),
                pltpu.VMEM(mod_table.shape, f32),
                pltpu.SMEM(timestep.shape, jnp.int32),
                pltpu.VMEM((HEADS, rows, dim), bf16),
                pltpu.VMEM((HEADS, rows, dim), bf16),
                pltpu.VMEM((rows, width), f32),
                pltpu.SemaphoreType.DMA,
                pltpu.SemaphoreType.DMA((sides, 2)),
                pltpu.SemaphoreType.DMA,
                pltpu.SemaphoreType.DMA((GROUPS,)),
                pltpu.SemaphoreType.DMA,
                pltpu.SemaphoreType.DMA,
                pltpu.SemaphoreType.DMA((sides, 2)),
                pltpu.SemaphoreType.DMA,
                pltpu.SemaphoreType.DMA,
                pltpu.SemaphoreType.DMA,
                pltpu.SemaphoreType.DMA,
            ],
            compiler_params=pltpu.CompilerParams(
                collective_id=0, has_side_effects=True, vmem_limit_bytes=60 * 1024 * 1024
            ),
        )(timestep, q_self, keys, values, q_cross, mod_table)

    placed = P("cam", "sp", None)
    return jax.shard_map(
        local,
        mesh=mesh,
        in_specs=(placed, placed, placed, placed, P(), P()),
        out_specs=placed,
        check_vma=False,
    )
```

time: 24.9 us -> 23.2 us (0.932)
  local copies, waits for them, and re-layouts: 1.57 us -> 0.66 us
  Pallas kernels: 22.6 us -> 21.7 us
    unnamed x1, local copies, waits for them, and re-layouts: 1.57 us -> 0.66 us
    pallas_call x1, Pallas kernels: 22.6 us -> 21.7 us  [local(): pl.pallas_call(functools.partial(kernel, n, cams), out_shape=pltpu.VMEM(q...]
where the time goes in v2:
time: 23.2 us; the launch traced here: 23.1 us
  Pallas kernels  21.7 us (94%)
  local copies, waits for them, and re-layouts  0.66 us (3%)
  between operations  0.66 us (3%)
    pallas_call x1, Pallas kernels, local(): pl.pallas_call(functools.partial(kernel, n, cams), out_shape=pltpu.VMEM(q...  21.7 us
    unnamed x1, local copies, waits for them, and re-layouts  0.66 us

profile of v2, /device:TPU:0, one launch (start us, length us, event | category | flops | bytes accessed | tf_op | source)
XLA Modules:
  0.0 23.1 jit_solution(10840525104570702640)
XLA Ops:
  0.7 21.7 %shard_map.64 = bf16[1,32,2048]{2,1,0:T(8,128)(2,1)S(1)} custom-call(s32[1]{0:T(128)S(6)} %copy.9.step_in, bf16[1,32,2048]{2,1,0:T(8,128)(2,1)} %q_ref.1, bf16[1,32,2048]{2,1,0:T(8,128)(2,1)} %k_ref.1, bf16[1,32,2048]{2,1,0:T(8,128)(2,1)} %v_ref.1, bf16[1,32,2048]{2,1,0:T(8,128)(2,1)} %qc_ref.1, f32[50,2,2048]{2,1,0:T(2,128)} %mod_ref.1), custom_call_target="tpu_custom_call" | custom-call | tf_op jit(solution)/shard_map/pallas_call | solution.py:179
  22.4 0.7 %copy.8 = bf16[1,32,2048]{2,1,0:T(8,128)(2,1)} copy(bf16[1,32,2048]{2,1,0:T(8,128)(2,1)S(1)} %shard_map.64) | data formatting | bytes 262144

commit v3 on v2

--- a/solution.py
+++ b/solution.py
@@ -14,8 +14,14 @@
 LOG2E = 1.4426950408889634
 
 
-def offsets(count):
-    return sorted(range(1, count), key=lambda d: (-abs(d - count // 2), d))
+def flipped(place, count):
+    bits = [1 << b for b in range(count.bit_length() - 1)]
+    moves = [bit * (1 - 2 * lax.rem(lax.div(place, bit), 2)) for bit in bits]
+
+    def at(d):
+        return place + sum(move for bit, move in zip(bits, moves) if d & bit)
+
+    return at
 
 
 def softmax_parts(scores, scale):
@@ -44,7 +50,10 @@
     my_group = lax.div(me, heads)
     my_slot = lax.rem(me, heads)
     scale = 1.0 / math.sqrt(dim)
-    order = offsets(heads) + [0]
+    peer_at = flipped(me, n)
+    target_at = flipped(my_slot, heads)
+    source_at = flipped(head, heads)
+    order = list(range(heads - 1, -1, -1))
     groups = q_sem.shape[0]
     per = heads // groups
 
@@ -52,10 +61,8 @@
         return pl.ds(pl.multiple_of(h * dim, dim), dim)
 
     barrier = pltpu.get_barrier_semaphore()
-    for d in offsets(n):
-        pl.semaphore_signal(
-            barrier, inc=1, device_id={"sp": lax.rem(me + d, n)}, device_id_type=MESH
-        )
+    for d in range(1, n):
+        pl.semaphore_signal(barrier, inc=1, device_id={"sp": peer_at(d)}, device_id_type=MESH)
     for side in range(sides):
         other = lax.rem(cam + (1 if side == 0 else cams - 1), cams)
         pl.semaphore_signal(barrier, inc=1, device_id={"cam": other}, device_id_type=MESH)
@@ -76,9 +83,9 @@
             device_id={"sp": peer}, device_id_type=MESH,
         ).start()
 
-    for src, dst, sem in ((k_ref, k_all, k_sem), (v_ref, v_all, v_sem)):
-        for d in offsets(n):
-            peer = lax.rem(me + d, n)
+    for d in range(1, n):
+        peer = peer_at(d)
+        for src, dst, sem in ((k_ref, k_all, k_sem), (v_ref, v_all, v_sem)):
             send(src.at[0, :, cols(lax.div(peer, copies))], dst.at[me], sem, peer)
 
     def by_place(d, peer, far, near):
@@ -89,7 +96,7 @@
             pl.when(peer == me)(near)
 
     for i, d in enumerate(order):
-        target = lax.rem(my_slot + d, heads)
+        target = target_at(d)
         peer = target * copies + my_group
         src, dst, sem = q_ref.at[0, :, cols(target)], q_all.at[i], q_sem.at[i // per]
         by_place(
@@ -118,15 +125,16 @@
         mine[here] = result.astype(jnp.bfloat16).reshape(per, rows, dim)
         for i in range(g * per, (g + 1) * per):
             d = order[i]
-            peer = copy * heads + lax.rem(head + heads - d, heads)
-            src, dst = mine.at[i], back.at[head]
+            peer = copy * heads + source_at(d)
+            src, dst = mine.at[i], back.at[i]
+            sem = back_sem.at[g]
             by_place(
                 d, peer,
                 lambda: pltpu.make_async_remote_copy(
-                    src_ref=src, dst_ref=dst, send_sem=back_send, recv_sem=back_sem,
+                    src_ref=src, dst_ref=dst, send_sem=back_send, recv_sem=sem,
                     device_id={"sp": peer}, device_id_type=MESH,
                 ).start(),
-                lambda: pltpu.make_async_copy(src, dst, back_sem).start(),
+                lambda: pltpu.make_async_copy(src, dst, sem).start(),
             )
 
     load_qc.wait()
@@ -144,11 +152,14 @@
         result = jnp.dot(w, vals, preferred_element_type=jnp.float32) / total
         cross[:, part] = gates[1:2, part] * result
 
-    pltpu.make_async_copy(back, back, back_sem).wait()
-    for h in range(heads):
-        part = slice(h * dim, (h + 1) * dim)
-        mixed = gates[0:1, part] * back[h].astype(jnp.float32) + cross[:, part]
-        out_ref[0, :, part] = mixed.astype(out_ref.dtype)
+    for g in range(groups):
+        here = pl.ds(g * per, per)
+        pltpu.make_async_copy(back.at[here], back.at[here], back_sem.at[g]).wait()
+        for i in range(g * per, (g + 1) * per):
+            part = cols(target_at(order[i]))
+            gate = mod[step_ref[0], :, part][0:1]
+            mixed = gate * back[i].astype(jnp.float32) + cross[:, part]
+            out_ref[0, :, part] = mixed.astype(out_ref.dtype)
 
     for dst in (k_all, v_all):
         sent = dst.at[pl.ds(0, n - 1)]
@@ -200,7 +211,7 @@
                 pltpu.SemaphoreType.DMA,
                 pltpu.SemaphoreType.DMA,
                 pltpu.SemaphoreType.DMA((sides, 2)),
-                pltpu.SemaphoreType.DMA,
+                pltpu.SemaphoreType.DMA((GROUPS,)),
                 pltpu.SemaphoreType.DMA,
                 pltpu.SemaphoreType.DMA,
                 pltpu.SemaphoreType.DMA,

time: 23.2 us -> 22.6 us (0.974)
  Pallas kernels: 21.7 us -> 21.1 us
    pallas_call x1, Pallas kernels: 21.7 us -> 21.1 us  [local(): pl.pallas_call(functools.partial(kernel, n, cams), out_shape=pltpu.VMEM(q...]
where the time goes in v3:
time: 22.6 us; the launch traced here: 22.4 us
  Pallas kernels  21.1 us (93%)
  local copies, waits for them, and re-layouts  0.66 us (3%)
  between operations  0.66 us (3%)
    pallas_call x1, Pallas kernels, local(): pl.pallas_call(functools.partial(kernel, n, cams), out_shape=pltpu.VMEM(q...  21.1 us
    unnamed x1, local copies, waits for them, and re-layouts  0.66 us

profile of v3, /device:TPU:0, one launch (start us, length us, event | category | flops | bytes accessed | tf_op | source)
XLA Modules:
  0.0 22.4 jit_solution(17099121509650420434)
XLA Ops:
  0.7 21.1 %shard_map.64 = bf16[1,32,2048]{2,1,0:T(8,128)(2,1)S(1)} custom-call(s32[1]{0:T(128)S(6)} %copy.9.step_in, bf16[1,32,2048]{2,1,0:T(8,128)(2,1)} %q_ref.1, bf16[1,32,2048]{2,1,0:T(8,128)(2,1)} %k_ref.1, bf16[1,32,2048]{2,1,0:T(8,128)(2,1)} %v_ref.1, bf16[1,32,2048]{2,1,0:T(8,128)(2,1)} %qc_ref.1, f32[50,2,2048]{2,1,0:T(2,128)} %mod_ref.1), custom_call_target="tpu_custom_call" | custom-call | tf_op jit(solution)/shard_map/pallas_call | solution.py:190
  21.8 0.7 %copy.8 = bf16[1,32,2048]{2,1,0:T(8,128)(2,1)} copy(bf16[1,32,2048]{2,1,0:T(8,128)(2,1)S(1)} %shard_map.64) | data formatting | bytes 262144
